TPU v7x, 32 devices: a whole 2x2x4 slice. The times are simulated.
32 devices in a mesh: dp: 16 (over z, y, x), mp: 2 (over core).
Axes of the slice: x: 2, y: 2, z: 4, core: 2. Of those that a mesh axis runs over, the one named last changes fastest.
Arguments:
- tokens: bfloat16 [18464, 768], P('dp'), may hold values from -6 to 6
- row_ids: int32 [18464], P('dp'), may hold values from 0 to 31, as said below
- select: int32 [18464], P('dp'), may hold values 0 or 1
- priority: int32 [18464], P('dp'), may hold values from 0 to 1153, as said below
- first_gain: float32 [768], replicated, may hold values from 0.5 to 1.5
- first_shift: float32 [768], replicated, may hold values from -1 to 1
- router: float32 [768], replicated, may hold values from -0.21875 to 0.21875
- w_attend: bfloat16 [768, 3, 768], P(None, None, 'mp'), may hold values from -0.21875 to 0.21875
- w_output: bfloat16 [768, 768], P('mp'), may hold values from -3 to 3
- second_gain: float32 [768], replicated, may hold values from 0.5 to 1.5
- second_shift: float32 [768], replicated, may hold values from -1 to 1
- w_expand: bfloat16 [768, 3072], P(None, 'mp'), may hold values from -0.21875 to 0.21875
- w_reduce: bfloat16 [3072, 768], P('mp'), may hold values from -0.109375 to 0.109375
- cotangent: bfloat16 [18464, 768], P('dp'), may hold values from -6 to 6
Outputs:
- layer_out: bfloat16 [18464, 768], P('dp')
- tokens_grad: float32 [18464, 768], P('dp')
- first_gain_grad: float32 [768], P('dp')
- first_shift_grad: float32 [768], P('dp')
- router_grad: float32 [768], P('dp')
- attend_grad: float32 [768, 3, 768], P('dp', None, 'mp')
- output_grad: float32 [768, 768], P('mp', 'dp')
- second_gain_grad: float32 [768], P('dp')
- second_shift_grad: float32 [768], P('dp')
- expand_grad: float32 [768, 3072], P('dp', 'mp')
- reduce_grad: float32 [3072, 768], P('mp', 'dp')
Inputs may be any that keep to these rules, and one draw needn't show every extreme that they name: `row_ids`: each of the 32 rows has 577 tokens, and every index of dp holds 36 or one more of every row's tokens. `priority`: on each index of dp the 1154 values are a permutation.
All inputs are finite; a program needn't handle non-finite values. No bound on the sum of `select` on one device may be relied on, other than what follows from the above.
Results may differ from a plain program's by a relative error of at most 0.015.
Values may be sent and summed in bfloat16 or wider, within the bound.
A program may use at most 192 MiB of HBM per device.

v0:
```python
import jax
import jax.numpy as jnp
from jax import lax
from jax.sharding import PartitionSpec as P

HD = 64
ROW_LEN = 577
ROWS_DEV = 2


EPSILON = 1e-06
MASKED_SCORE = -1000000000.0


def layer_norm(value, gain, shift):
    center = value - jnp.mean(value, axis=-1, keepdims=True)
    spread = jnp.mean(center * center, axis=-1, keepdims=True)
    return center * lax.rsqrt(spread + EPSILON) * gain + shift


def gelu_exact(value):
    return jax.nn.gelu(value, approximate=False)


def split_heads(proj_rows, which):
    slot_count = proj_rows.shape[1]
    return proj_rows[which].reshape(slot_count, proj_rows.shape[2] // HD, HD)


def head_scores(proj_rows, valid_keys):
    scores = jnp.einsum(
        "qhd,khd->hqk",
        split_heads(proj_rows, 0),
        split_heads(proj_rows, 1),
        preferred_element_type=jnp.float32,
    ) * HD ** (-0.5)
    return jnp.where(valid_keys[None, None, :], scores, MASKED_SCORE)


def row_forward(buffer, valid_keys, w_attend):
    proj_rows = jnp.einsum(
        "sd,dch->csh", buffer, w_attend, preferred_element_type=jnp.float32
    ).astype(jnp.bfloat16)
    scores = head_scores(proj_rows, valid_keys)
    row_peak = jnp.max(scores, axis=-1, keepdims=True)
    weights = jnp.exp(scores - row_peak)
    exp_total = jnp.sum(weights, axis=-1, keepdims=True)
    probs_low = (weights / exp_total).astype(jnp.bfloat16)
    context = jnp.einsum(
        "hqk,khd->qhd", probs_low, split_heads(proj_rows, 2), preferred_element_type=jnp.float32
    )
    context = context.reshape(buffer.shape[0], -1).astype(jnp.bfloat16)
    return (context, (row_peak + jnp.log(exp_total))[..., 0], proj_rows)


def row_backward(buffer, valid_keys, proj_rows, log_total, context_grad, w_attend):
    slot_count = buffer.shape[0]
    scores = head_scores(proj_rows, valid_keys)
    probs = jnp.exp(scores - log_total[..., None])
    upstream = context_grad.reshape(slot_count, -1, HD)
    probs_grad = jnp.einsum(
        "qhd,khd->hqk", upstream, split_heads(proj_rows, 2), preferred_element_type=jnp.float32
    )
    row_delta = jnp.sum(probs * probs_grad, axis=-1, keepdims=True)
    scores_grad = (probs * (probs_grad - row_delta)).astype(jnp.bfloat16)
    value_grad = jnp.einsum(
        "hqk,qhd->khd", probs.astype(jnp.bfloat16), upstream, preferred_element_type=jnp.float32
    )
    query_grad = jnp.einsum(
        "hqk,khd->qhd", scores_grad, split_heads(proj_rows, 1), preferred_element_type=jnp.float32
    ) * HD ** (-0.5)
    key_grad = jnp.einsum(
        "hqk,qhd->khd", scores_grad, split_heads(proj_rows, 0), preferred_element_type=jnp.float32
    ) * HD ** (-0.5)
    proj_grad = jnp.stack(
        [
            query_grad.reshape(slot_count, -1),
            key_grad.reshape(slot_count, -1),
            value_grad.reshape(slot_count, -1),
        ]
    ).astype(jnp.bfloat16)
    buffer_grad = jnp.einsum("csh,dch->sd", proj_grad, w_attend, preferred_element_type=jnp.float32)
    attend_term = jnp.einsum("sd,csh->dch", buffer, proj_grad, preferred_element_type=jnp.float32)
    return (buffer_grad, attend_term)


def shards(
    tokens,
    row_ids,
    select,
    priority,
    first_gain,
    first_shift,
    router,
    w_attend,
    w_output,
    second_gain,
    second_shift,
    w_expand,
    w_reduce,
    cotangent,
):
    dp_count = lax.axis_size("dp")
    capacity = 5 * ROW_LEN // (8 * dp_count)
    send_slots = ROWS_DEV * dp_count * capacity
    model_width = tokens.shape[1]
    head_cols = w_attend.shape[2]
    owner_dev = row_ids // ROWS_DEV
    local_row = row_ids % ROWS_DEV
    same_row = row_ids[:, None] == row_ids[None, :]
    earlier = priority[None, :] < priority[:, None]
    ranking = jnp.sum((same_row & earlier & (select[None, :] == 1)).astype(jnp.int32), axis=1)
    kept_mask = (select == 1) & (ranking < capacity)
    slot_index = (local_row * dp_count + owner_dev) * capacity + jnp.minimum(ranking, capacity - 1)
    dispatch = (
        (jnp.arange(send_slots, dtype=jnp.int32)[:, None] == slot_index[None, :])
        & kept_mask[None, :]
    ).astype(jnp.bfloat16)

    def collect(returned, width):
        picked = jnp.take(returned.reshape(send_slots, width), slot_index, axis=0)
        return jnp.where(kept_mask[:, None], picked, jnp.zeros((), picked.dtype))

    tokens_wide = tokens.astype(jnp.float32)
    first_value, first_pull = jax.vjp(layer_norm, tokens_wide, first_gain, first_shift)
    normed = first_value.astype(jnp.bfloat16)
    gate_value = jax.nn.sigmoid(jnp.sum(normed.astype(jnp.float32) * router, axis=-1))
    send_buffer = (
        jnp.dot(dispatch, normed, preferred_element_type=jnp.float32)
        .astype(jnp.bfloat16)
        .reshape(ROWS_DEV, dp_count, capacity, model_width)
    )
    send_flags = (
        jnp.sum(dispatch, axis=1, dtype=jnp.float32)
        .astype(jnp.bfloat16)
        .reshape(ROWS_DEV, dp_count, capacity)
    )
    buffers = lax.all_to_all(send_buffer, "dp", split_axis=1, concat_axis=1, tiled=True)
    slot_flags = lax.all_to_all(send_flags, "dp", split_axis=1, concat_axis=1, tiled=True)
    item_count = buffers.shape[0]
    buffers = buffers.reshape(item_count, -1, model_width)
    valid_keys = slot_flags.reshape(item_count, -1) > 0.5
    context, log_total, proj_rows = lax.map(
        lambda element: row_forward(element[0], element[1], w_attend), (buffers, valid_keys)
    )
    context = context.reshape(item_count, dp_count, capacity, head_cols)
    partial_out = jnp.einsum("knch,hd->kncd", context, w_output, preferred_element_type=jnp.float32)
    forward_out = (buffers, valid_keys, proj_rows, log_total, context, partial_out)
    buffers = forward_out[0]
    valid_keys = forward_out[1]
    proj_rows = forward_out[2]
    log_total = forward_out[3]
    context = forward_out[4]
    returned = lax.all_to_all(
        forward_out[5].astype(jnp.bfloat16), "dp", split_axis=1, concat_axis=1, tiled=True
    ).astype(jnp.float32)
    attend_part = collect(returned, model_width)
    attended = lax.psum(attend_part.astype(jnp.bfloat16), "mp").astype(jnp.float32)
    mixed_rows = tokens_wide + gate_value[:, None] * attended
    second_value, second_pull = jax.vjp(layer_norm, mixed_rows, second_gain, second_shift)
    hidden_two = second_value.astype(jnp.bfloat16)
    pre_act = jnp.dot(hidden_two, w_expand, preferred_element_type=jnp.float32)
    gelu_value, gelu_pull = jax.vjp(gelu_exact, pre_act)
    activated = gelu_value.astype(jnp.bfloat16)
    mlp_out = lax.psum(
        jnp.dot(activated, w_reduce, preferred_element_type=jnp.float32).astype(jnp.bfloat16), "mp"
    ).astype(jnp.float32)
    layer_out = (mixed_rows + mlp_out).astype(jnp.bfloat16)
    act_grad = jnp.einsum("td,fd->tf", cotangent, w_reduce, preferred_element_type=jnp.float32)
    reduce_grad = jnp.einsum("tf,td->fd", activated, cotangent, preferred_element_type=jnp.float32)
    pre_grad = gelu_pull(act_grad)[0].astype(jnp.bfloat16)
    expand_grad = jnp.einsum("td,tf->df", hidden_two, pre_grad, preferred_element_type=jnp.float32)
    hidden_grad = lax.psum(
        jnp.einsum("tf,df->td", pre_grad, w_expand, preferred_element_type=jnp.float32).astype(
            jnp.bfloat16
        ),
        "mp",
    ).astype(jnp.float32)
    mixed_part, second_gain_grad, second_shift_grad = second_pull(hidden_grad)
    mixed_grad = cotangent.astype(jnp.float32) + mixed_part
    attended_grad = (mixed_grad * gate_value[:, None]).astype(jnp.bfloat16)
    logit_grad = jnp.sum(mixed_grad * attended, axis=-1) * gate_value * (1.0 - gate_value)
    router_grad = jnp.sum(logit_grad[:, None] * normed.astype(jnp.float32), axis=0)
    sent_grads = (
        jnp.dot(dispatch, attended_grad, preferred_element_type=jnp.float32)
        .astype(jnp.bfloat16)
        .reshape(ROWS_DEV, dp_count, capacity, model_width)
    )
    at_owner = lax.all_to_all(sent_grads, "dp", split_axis=1, concat_axis=1, tiled=True)
    context_grad = jnp.einsum(
        "kncd,hd->knch", at_owner, w_output, preferred_element_type=jnp.float32
    ).astype(jnp.bfloat16)
    output_grad = jnp.einsum("knch,kncd->hd", context, at_owner, preferred_element_type=jnp.float32)
    buffer_grad, attend_terms = lax.map(
        lambda element: row_backward(
            element[0], element[1], element[2], element[3], element[4], w_attend
        ),
        (buffers, valid_keys, proj_rows, log_total, context_grad.reshape(ROWS_DEV, -1, head_cols)),
    )
    attend_grad = jnp.sum(attend_terms, axis=0)
    returned_grad = lax.all_to_all(
        buffer_grad.reshape(ROWS_DEV, dp_count, capacity, model_width).astype(jnp.bfloat16),
        "dp",
        split_axis=1,
        concat_axis=1,
        tiled=True,
    ).astype(jnp.float32)
    normed_grad = (
        lax.psum(collect(returned_grad, model_width).astype(jnp.bfloat16), "mp").astype(jnp.float32)
        + logit_grad[:, None] * router
    )
    token_part, first_gain_grad, first_shift_grad = first_pull(normed_grad)
    tokens_grad = mixed_grad + token_part
    row_parts = (
        lax.psum_scatter(attend_grad, "dp", scatter_dimension=0, tiled=True),
        lax.psum_scatter(expand_grad, "dp", scatter_dimension=0, tiled=True),
        lax.psum_scatter(first_gain_grad, "dp", scatter_dimension=0, tiled=True),
        lax.psum_scatter(first_shift_grad, "dp", scatter_dimension=0, tiled=True),
        lax.psum_scatter(router_grad, "dp", scatter_dimension=0, tiled=True),
        lax.psum_scatter(second_gain_grad, "dp", scatter_dimension=0, tiled=True),
        lax.psum_scatter(second_shift_grad, "dp", scatter_dimension=0, tiled=True),
    )
    column_parts = (
        lax.psum_scatter(output_grad, "dp", scatter_dimension=1, tiled=True),
        lax.psum_scatter(reduce_grad, "dp", scatter_dimension=1, tiled=True),
    )
    return (
        layer_out,
        tokens_grad,
        row_parts[2],
        row_parts[3],
        row_parts[4],
        row_parts[0],
        column_parts[0],
        row_parts[5],
        row_parts[6],
        row_parts[1],
        column_parts[1],
    )


def solution(mesh):
    in_specs = (
        P("dp", None),
        P("dp"),
        P("dp"),
        P("dp"),
        P(),
        P(),
        P(),
        P(None, None, "mp"),
        P("mp", None),
        P(),
        P(),
        P(None, "mp"),
        P("mp", None),
        P("dp", None),
    )
    out_specs = (
        P("dp", None),
        P("dp", None),
        P("dp"),
        P("dp"),
        P("dp"),
        P("dp", None, "mp"),
        P("mp", "dp"),
        P("dp"),
        P("dp"),
        P("dp", "mp"),
        P("mp", "dp"),
    )
    return jax.shard_map(shards, mesh=mesh, in_specs=in_specs, out_specs=out_specs, check_vma=False)
```

profile of v0, /device:TPU:0, one launch (start us, length us, event | category | flops | bytes accessed | tf_op | source)
XLA Modules:
  0.0 950.1 jit_solution(2436582117340358125)
XLA Ops:
  8.1 2.7 convert_reduce_fusion
  13.6 8.4 all-to-all-start.1
  29.3 3.1 fusion.65
  35.8 7.1 all-to-all-start
  43.8 23.6 %all-to-all-done = bf16[2,16,22,768]{3,0,2,1:T(2,128)(2,1)S(1)} async-done(((bf16[2,16,22,768]{3,0,2,1:T(2,128)(2,1)}), bf16[2,16,22,768]{3,0,2,1:T(2,128)(2,1)S(1)}, u32[]{:S(2)}, u32[]{:S(2)}) %all-to-all-start) | async-done | bytes 1081376 | tf_op jit(solution)/shard_map/all_to_all | solution.py:138
  69.7 18.8 %while.26 = (s32[]{:T(128)}, bf16[2,352,384]{1,2,0:T(8,128)(2,1)}, f32[2,6,352]{2,1,0:T(8,128)}, bf16[2,3,352,384]{3,2,1,0:T(8,128)(2,1)}, bf16[2,352,768]{2,1,0...) while((s32[]{:T(128)}, bf16[2,352,384]{1,2,0:T(8,128)(2,1)}, ...), condition=%wide.region_8.9_spmd, body=%wide.region_5.8_spmd.sunk | while | flops 822630336 | bytes 31900372 | solution.py:143
  69.8 3.6 bitcast_dynamic-update-slice_fusion.6
  79.2 3.6 bitcast_dynamic-update-slice_fusion.6
  88.5 3.2 copy.217
  95.8 5.9 all-to-all-start.2
  101.9 23.6 %all-to-all-done.2 = bf16[2,16,22,768]{3,0,2,1:T(2,128)(2,1)} async-done(((bf16[2,16,22,768]{3,0,2,1:T(2,128)(2,1)}), bf16[2,16,22,768]{3,0,2,1:T(2,128)(2,1)}, u32[]{:S(2)}, u32[]{:S(2)}) %all-to-all-start.2) | async-done | bytes 1081376 | tf_op jit(solution)/shard_map/all_to_all | solution.py:154
  129.5 4.8 gather_fusion
  134.4 3.0 fusion.47
  137.5 21.2 %all-reduce.11.cloned.1.call-done = bf16[1154,768]{1,0:T(8,128)(2,1)} async-done(((bf16[1154,768]{1,0:T(8,128)(2,1)}), bf16[1154,768]{1,0:T(8,128)(2,1)}) %all-reduce.11.cloned.1.call-update) | async-done | bytes 1772560 | tf_op jit(solution)/shard_map/psum | solution.py:158
  158.8 3.0 fusion.57
  163.1 3.7 fusion.89
  166.9 20.2 %add_convert_fusion = (bf16[1154,1536]{1,0:T(8,128)(2,1)S(1)}, f32[1154,1536]{1,0:T(8,128)}) fusion(f32[1154,1536]{1,0:T(8,128)S(1)} %fusion.89, bf16[1154,768]{1,0:T(8,128)(2,1)S(1)} %copy-done.24, bf16[1536,768]{1,0:T(8,128)(2,1)S(1)} %copy-done), kind=kOutput, calls=%fused_computation.46 | convolution fusion | flops 2850250752 | bytes 21857280 | tf_op jit(solution)/shard_map/td,fd->tf/dot_general | solution.py:169
  188.8 4.1 convolution_convert_fusion.1
  193.0 22.1 %all-reduce.13.cloned.1.call-done = bf16[1154,768]{1,0:T(8,128)(2,1)} async-done(((bf16[1154,768]{1,0:T(8,128)(2,1)}), bf16[1154,768]{1,0:T(8,128)(2,1)}) %all-reduce.13.cloned.1.call-update) | async-done | bytes 1772560 | tf_op jit(solution)/shard_map/psum | solution.py:173
  215.1 5.1 convert_reduce_fusion.1
  220.3 3.5 fusion.45
  223.8 3.8 fusion.42
  229.4 3.2 fusion.68
  236.2 6.8 all-to-all-start.3
  243.1 25.3 %all-to-all-done.3 = bf16[2,16,22,768]{3,0,2,1:T(2,128)(2,1)S(1)} async-done(((bf16[2,16,22,768]{3,0,2,1:T(2,128)(2,1)}), bf16[2,16,22,768]{3,0,2,1:T(2,128)(2,1)S(1)}, u32[]{:S(2)}, u32[]{:S(2)}) %all-to-all-start.3) | async-done | bytes 1081376 | tf_op jit(solution)/shard_map/all_to_all | solution.py:189
  274.2 47.0 %while.27 = (s32[]{:T(128)}, bf16[2,352,768]{2,1,0:T(8,128)(2,1)}, f32[2,768,3,384]{3,1,2,0:T(8,128)}, bf16[2,3,352,384]{3,2,1,0:T(8,128)(2,1)}, pred[2,352]{1,0...) while((s32[]{:T(128)}, bf16[2,352,768]{2,1,0:T(8,128)(2,1)}, ...), condition=%wide.region_18.20_spmd, body=%wide.region_16.19_spmd.sunk | while | flops 1732108288 | bytes 50904704 | solution.py:194
  290.2 3.3 fusion.172
  293.6 4.2 bitcast_dynamic-update-slice_fusion.8
  313.8 3.3 fusion.172
  317.0 4.1 bitcast_dynamic-update-slice_fusion.8
  321.2 3.4 copy.228
  324.6 6.7 all-to-all-start.4
  331.5 6.9 multiply_convert_fusion.1
  340.3 4.0 convolution_convert_fusion.2
  344.4 11.1 %all-to-all-done.4 = bf16[2,16,22,768]{3,0,2,1:T(2,128)(2,1)S(1)} async-done(((bf16[2,16,22,768]{3,0,2,1:T(2,128)(2,1)}), bf16[2,16,22,768]{3,0,2,1:T(2,128)(2,1)S(1)}, u32[]{:S(2)}, u32[]{:S(2)}) %all-to-all-start.4) | async-done | bytes 1081376 | tf_op jit(solution)/shard_map/all_to_all | solution.py:201
  358.3 4.9 gather_fusion.1
  363.2 3.1 fusion.46
  366.5 2.9 convolution_bitcast_fusion.1
  369.5 8.0 fusion.97
  378.2 9.5 fusion.88
  387.8 6.1 reduce_sum.230
  395.9 4.3 fusion.48
  402.9 76.5 %all-reduce.5 = (f32[768]{0:T(1024)S(1)}, f32[768]{0:T(1024)S(1)}, f32[768]{0:T(1024)S(1)}, f32[768]{0:T(1024)S(1)}, f32[768]{0:T(1024)S(1)}) all-reduce(f32[768]{0:T(1024)S(1)} %get-tuple-element.227, f32[768]{0:T(1024)S(1)} %get-tuple-element.229, f32[768]{0:T(1024)S(1)} %get-tuple-element.233, ...), channel_id=2, replica_groups=mesh['dp'=16,'mp'=2] {'dp'}, use_global_device_ids=true, to_apply=%region_24.26.clone | all-reduce | flops 3840 | bytes 30720
  482.3 6.7 add_add_fusion.2
  489.0 31.9 %reduce-scatter.7.cloned.1.call-done = f32[384,48]{0,1:T(8,128)} async-done(((f32[384,768]{0,1:T(8,128)}), f32[384,48]{0,1:T(8,128)}) %reduce-scatter.7.cloned.1.call-update) | async-done | bytes 73744 | tf_op jit(solution)/shard_map/reduce_scatter | solution.py:224
  520.9 141.6 %reduce-scatter.11.cloned.1.call-done = f32[1536,48]{0,1:T(8,128)} async-done(((f32[1536,768]{0,1:T(8,128)}), f32[1536,48]{0,1:T(8,128)}) %reduce-scatter.11.cloned.1.call-update) | async-done | bytes 294928 | tf_op jit(solution)/shard_map/reduce_scatter | solution.py:225
  662.5 141.8 %reduce-scatter.9.cloned.1.call-done = f32[48,1536]{1,0:T(8,128)} async-done(((f32[768,1536]{1,0:T(8,128)}), f32[48,1536]{1,0:T(8,128)}) %reduce-scatter.9.cloned.1.call-update) | async-done | bytes 294928 | tf_op jit(solution)/shard_map/reduce_scatter | solution.py:216
  804.3 138.5 %reduce-scatter.5.cloned.1.call-done = f32[48,3,384]{2,0,1:T(8,128)} async-done(((f32[768,3,384]{2,0,1:T(8,128)}), f32[48,3,384]{2,0,1:T(8,128)}) %reduce-scatter.5.cloned.1.call-update) | async-done | bytes 221200 | tf_op jit(solution)/shard_map/reduce_scatter | solution.py:215
  (276 shorter events, 96.2 us)
Async XLA Ops:
  7.2 159.7 %copy-start = (bf16[1536,768]{1,0:T(8,128)(2,1)S(1)}, bf16[1536,768]{1,0:T(8,128)(2,1)}, u32[]{:S(2)}) copy-start(bf16[1536,768]{1,0:T(8,128)(2,1)} %param.32) | copy-start | bytes 7077892
  7.2 19.5 %copy-start.48 = (f32[768]{0:T(1024)S(1)}, f32[768]{0:T(1024)}, u32[]{:S(2)}) copy-start(f32[768]{0:T(1024)} %param.26) | copy-start | bytes 9220
  7.2 19.5 %copy-start.50 = (f32[768]{0:T(1024)S(1)}, f32[768]{0:T(1024)}, u32[]{:S(2)}) copy-start(f32[768]{0:T(1024)} %param.24) | copy-start | bytes 9220
  7.2 19.5 %copy-start.61 = (f32[768]{0:T(1024)S(1)}, f32[768]{0:T(1024)}, u32[]{:S(2)}) copy-start(f32[768]{0:T(1024)} %param.25) | copy-start | bytes 9220
  12.0 16.0 %copy-start.44 = (s32[1154]{0:T(1024)}, s32[1154]{0:T(1024)S(1)}, u32[]{:S(2)}) copy-start(s32[1154]{0:T(1024)S(1)} %get-tuple-element.280) | copy-start | bytes 13852
  12.0 215.5 %copy-start.54 = (pred[1154]{0:T(1024)(128)(4,1)}, pred[1154]{0:T(1024)(128)(4,1)S(1)}, u32[]{:S(2)}) copy-start(pred[1154]{0:T(1024)(128)(4,1)S(1)} %get-tuple-element.295) | copy-start | bytes 3466
  13.6 22.2 %all-to-all-start.1 = ((bf16[2,16,22]{2,0,1:T(2,128)(2,1)}), bf16[2,16,22]{2,0,1:T(2,128)(2,1)}, u32[]{:S(2)}, u32[]{:S(2)}) async-start(bf16[2,16,22]{2,0,1:T(2,128)(2,1)} %copy.214), calls=%async_computation.1 | async-start | bytes 16384 | tf_op jit(solution)/shard_map/all_to_all | solution.py:139
  22.0 4.7 copy-start.1
  23.9 4.1 copy-start.32
  28.0 109.5 %copy-start.42 = (f32[1154]{0:T(1024)}, f32[1154]{0:T(1024)S(1)}, u32[]{:S(2)}) copy-start(f32[1154]{0:T(1024)S(1)} %get-tuple-element.277) | copy-start | bytes 13852
  35.8 31.6 %all-to-all-start = ((bf16[2,16,22,768]{3,0,2,1:T(2,128)(2,1)}), bf16[2,16,22,768]{3,0,2,1:T(2,128)(2,1)S(1)}, u32[]{:S(2)}, u32[]{:S(2)}) async-start(bf16[2,16,22,768]{3,0,2,1:T(2,128)(2,1)} %copy.213), calls=%async_computation | async-start | bytes 2162688 | tf_op jit(solution)/shard_map/all_to_all | solution.py:138
  88.5 7.3 copy-start.12
  91.7 10.1 %copy-start.45 = (s32[1154]{0:T(1024)S(1)}, s32[1154]{0:T(1024)}, u32[]{:S(2)}) copy-start(s32[1154]{0:T(1024)} %copy-done.44) | copy-start | bytes 13852
  95.8 29.6 %all-to-all-start.2 = ((bf16[2,16,22,768]{3,0,2,1:T(2,128)(2,1)}), bf16[2,16,22,768]{3,0,2,1:T(2,128)(2,1)}, u32[]{:S(2)}, u32[]{:S(2)}) async-start(bf16[2,16,22,768]{3,0,2,1:T(2,128)(2,1)} %copy.219), calls=%async_computation.2 | async-start | bytes 2162688 | tf_op jit(solution)/shard_map/all_to_all | solution.py:154
  101.8 57.0 %all-reduce.11.cloned.1.call-start = ((), (), s32[]{:S(2)}) async-start(), calls=%async_computation.9 | async-start | bytes 3563520 | tf_op jit(solution)/shard_map/psum | solution.py:158
  101.8 32.5 %copy-start.38 = (s32[2048]{0:T(1024)}, s32[2048]{0:T(1024)S(1)}, u32[]{:S(2)}) copy-start(s32[2048]{0:T(1024)S(1)} %pad_clamp_fusion) | copy-start | bytes 24580
  129.5 4.8 copy-start.57
  137.4 77.6 %all-reduce.13.cloned.1.call-start = ((), (), s32[]{:S(2)}) async-start(), calls=%async_computation.10 | async-start | bytes 3563520 | tf_op jit(solution)/shard_map/psum | solution.py:173
  137.5 90.0 %copy-start.30 = (f32[1154]{0:T(1024)}, f32[1154]{0:T(1024)S(1)}, u32[]{:S(2)}) copy-start(f32[1154]{0:T(1024)S(1)} %add_divide_fusion) | copy-start | bytes 13852
  137.5 25.6 %copy-start.52 = (f32[768]{0:T(1024)S(1)}, f32[768]{0:T(1024)}, u32[]{:S(2)}) copy-start(f32[768]{0:T(1024)} %param.29) | copy-start | bytes 9220
  137.5 25.6 %copy-start.63 = (f32[768]{0:T(1024)S(1)}, f32[768]{0:T(1024)}, u32[]{:S(2)}) copy-start(f32[768]{0:T(1024)} %param.30) | copy-start | bytes 9220
  158.8 4.3 copy-start.62
  161.9 61.9 %copy-start.34 = (f32[1154]{0:T(1024)}, f32[1154]{0:T(1024)S(1)}, u32[]{:S(2)}) copy-start(f32[1154]{0:T(1024)S(1)} %broadcast_multiply_fusion) | copy-start | bytes 13852
  163.1 60.7 %copy-start.46 = (f32[1154]{0:T(1024)}, f32[1154]{0:T(1024)S(1)}, u32[]{:S(2)}) copy-start(f32[1154]{0:T(1024)S(1)} %fusion.86) | copy-start | bytes 13852
  166.9 20.2 %copy-start.17 = (f32[1154,1536]{1,0:T(8,128)}, f32[1154,1536]{1,0:T(8,128)S(1)}, u32[]{:S(2)}) copy-start(f32[1154,1536]{1,0:T(8,128)S(1)} %fusion.89) | copy-start | bytes 21270532
  215.1 5.2 copy-start.3
  215.1 5.2 copy-start.6
  215.1 5.2 copy-start.8
  236.2 32.1 %all-to-all-start.3 = ((bf16[2,16,22,768]{3,0,2,1:T(2,128)(2,1)}), bf16[2,16,22,768]{3,0,2,1:T(2,128)(2,1)S(1)}, u32[]{:S(2)}, u32[]{:S(2)}) async-start(bf16[2,16,22,768]{3,0,2,1:T(2,128)(2,1)} %copy.222), calls=%async_computation.3 | async-start | bytes 2162688 | tf_op jit(solution)/shard_map/all_to_all | solution.py:189
  284.7 5.5 copy-start.19
  293.6 4.2 copy-start.16
  308.2 5.5 copy-start.19
  317.0 4.2 copy-start.16
  324.6 30.9 %all-to-all-start.4 = ((bf16[2,16,22,768]{3,0,2,1:T(2,128)(2,1)}), bf16[2,16,22,768]{3,0,2,1:T(2,128)(2,1)S(1)}, u32[]{:S(2)}, u32[]{:S(2)}) async-start(bf16[2,16,22,768]{3,0,2,1:T(2,128)(2,1)} %bitcast.167), calls=%async_computation.4 | async-start | bytes 2162688 | tf_op jit(solution)/shard_map/all_to_all | solution.py:201
  331.3 64.5 %all-reduce.15.cloned.1.call-start = ((), (), s32[]{:S(2)}) async-start(), calls=%async_computation.15 | async-start | bytes 7127040 | tf_op jit(solution)/shard_map/psum | solution.py:165
  344.4 14.0 %copy-start.39 = (s32[2048]{0:T(1024)S(1)}, s32[2048]{0:T(1024)}, u32[]{:S(2)}) copy-start(s32[2048]{0:T(1024)} %copy-done.38) | copy-start | bytes 24580
  358.3 4.9 copy-start.55
  358.3 4.9 copy-start.58
  366.4 154.5 %reduce-scatter.7.cloned.1.call-start = ((), (), s32[]{:S(2)}) async-start(), calls=%async_computation.12 | async-start | bytes 1253376 | tf_op jit(solution)/shard_map/reduce_scatter | solution.py:224
  369.4 293.1 %reduce-scatter.11.cloned.1.call-start = ((), (), s32[]{:S(2)}) async-start(), calls=%async_computation.14 | async-start | bytes 5013504 | tf_op jit(solution)/shard_map/reduce_scatter | solution.py:225
  377.5 426.8 %reduce-scatter.9.cloned.1.call-start = ((), (), s32[]{:S(2)}) async-start(), calls=%async_computation.13 | async-start | bytes 5013504 | tf_op jit(solution)/shard_map/reduce_scatter | solution.py:216
  387.7 555.1 %reduce-scatter.5.cloned.1.call-start = ((), (), s32[]{:S(2)}) async-start(), calls=%async_computation.11 | async-start | bytes 3760128 | tf_op jit(solution)/shard_map/reduce_scatter | solution.py:215
  393.9 6.3 copy-start.41
  393.9 6.3 copy-start.37
  395.8 4.5 copy-start.4
  395.8 4.5 copy-start.7
  395.9 7.0 copy-start.59
  395.9 7.0 copy-start.60
  (42 other events, 77.0 us)
Sparse Core Ops, SparseCore 0:
  137.6 21.1 all-reduce.10
  193.1 21.8 all-reduce.12
  366.5 24.3 all-reduce.14
  396.1 124.7 reduce-scatter.6
  526.5 135.9 reduce-scatter.10
  668.9 135.3 reduce-scatter.8
  810.0 132.7 reduce-scatter.4
where the time goes:
time: 958 us; the launch traced here: 950 us
  waiting for transfers between devices  581 us (61%)
  matrix products  103 us (11%)
  blocking collectives  76.5 us (8%)
  local copies, waits for them, and re-layouts  70.5 us (7%)
  other arithmetic  67.2 us (7%)
  starting transfers between devices  35.6 us (4%)
  between operations  16 us (2%)
    reduce_scatter x1, waiting for transfers between devices, shards(): lax.psum_scatter(expand_grad, 'dp', scatter_dimension=0, tiled=True)  142 us
    reduce_scatter x1, waiting for transfers between devices, shards(): lax.psum_scatter(reduce_grad, 'dp', scatter_dimension=1, tiled=True)  142 us
    reduce_scatter x1, waiting for transfers between devices, shards(): lax.psum_scatter(attend_grad, 'dp', scatter_dimension=0, tiled=True)  139 us
    unnamed x1, blocking collectives  76.5 us
    reduce_scatter x1, waiting for transfers between devices, shards(): lax.psum_scatter(output_grad, 'dp', scatter_dimension=1, tiled=True)  31.9 us
    all_to_all x1, waiting for transfers between devices, shards(): lax.all_to_all(sent_grads, 'dp', split_axis=1, concat_axis=1, tiled=True)  25.3 us
    all_to_all x1, waiting for transfers between devices, shards(): lax.all_to_all(send_buffer, 'dp', split_axis=1, concat_axis=1, tiled=True)  23.6 us
    all_to_all x1, waiting for transfers between devices, shards(): lax.all_to_all(forward_out[5].astype(jnp.bfloat16), 'dp', split_axis=1, c...  23.6 us
  transfers between devices with their start and end apart: 12, of which 10 were waited for; matrix products, arithmetic and copies ran while one was open for 7% of the time, Pallas kernels for 0%

commit v1 on v0

v1 whole, which is shorter than its diff:
```python
import jax
import jax.numpy as jnp
from jax import lax
from jax.sharding import PartitionSpec as P

HD = 64
ROW_LEN = 577
EPSILON = 1e-06
MASKED_SCORE = -1000000000.0
EMPTY = 1e30
BF = jnp.bfloat16
F32 = jnp.float32


def mm(a, b, dims):
    return lax.dot_general(a, b, (dims, ((), ())), preferred_element_type=F32)


def norm_stats(value):
    center = value - jnp.mean(value, axis=-1, keepdims=True)
    inv = lax.rsqrt(jnp.mean(center * center, axis=-1, keepdims=True) + EPSILON)
    return center * inv, inv


def norm_pull(e, nhat, inv):
    return (e - jnp.mean(e, axis=-1, keepdims=True) - nhat * jnp.mean(e * nhat, axis=-1, keepdims=True)) * inv


def swap(value):
    return lax.ppermute(value, "mp", [(0, 1), (1, 0)])


def scatter_sum(grad, order):
    count = lax.axis_size("dp")
    me = lax.axis_index("dp")
    bits = count.bit_length() - 1
    width = grad.shape[0] // count
    dims = [2] * bits
    value = grad.reshape(dims + [width, grad.shape[1]])
    out = None
    for step in order:
        axis = bits - 1 - step
        mine = (me >> step) & 1
        give = lax.dynamic_slice_in_dim(value, 1 - mine, 1, axis)
        keep = lax.dynamic_slice_in_dim(value, mine, 1, axis)
        got = lax.ppermute(give, "dp", [(i, i ^ (1 << step)) for i in range(count)])
        out = keep.astype(F32) + got.astype(F32)
        value = out.astype(grad.dtype)
    return out.reshape(width, grad.shape[1])


def shards(
    tokens,
    row_ids,
    select,
    priority,
    first_gain,
    first_shift,
    router,
    w_attend,
    w_output,
    second_gain,
    second_shift,
    w_expand,
    w_reduce,
    cotangent,
):
    dp_count = lax.axis_size("dp")
    mp_count = lax.axis_size("mp")
    core = lax.axis_index("mp")
    bits = dp_count.bit_length() - 1
    order_a = list(range(bits))
    order_b = [1, 0] + list(range(2, bits))
    rows = dp_count * mp_count
    capacity = 5 * ROW_LEN // (8 * dp_count)
    half = capacity // mp_count
    count, width = tokens.shape
    own = count // mp_count
    slots = rows * half
    heads_cols = w_attend.shape[2]
    heads = heads_cols // HD

    w_attend_2 = (w_attend, swap(w_attend))
    w_output_2 = (w_output, swap(w_output))
    w_expand_2 = (w_expand, swap(w_expand))
    w_reduce_2 = (w_reduce, swap(w_reduce))

    chosen = select == 1
    same_row = row_ids[:, None] == row_ids[None, :]
    earlier = priority[None, :] < priority[:, None]
    rank = jnp.sum((same_row & earlier & chosen[None, :]).astype(jnp.int32), axis=1)
    kept = chosen & (rank < capacity)
    taken = jnp.sum(
        ((row_ids[None, :] == jnp.arange(rows)[:, None]) & kept[None, :]).astype(jnp.int32), axis=1
    )
    slot_of = (jnp.arange(mp_count) * half)[:, None, None] + jnp.arange(half)[None, None, :]
    filled = (slot_of < taken[None, :, None]).reshape(mp_count, slots)
    filled_all = jnp.pad(filled, ((0, 0), (0, own - slots))).reshape(count)
    place = jnp.where(
        kept,
        (rank // half) * own + row_ids * half + rank % half,
        count + jnp.cumsum(jnp.where(kept, 0, 1)),
    )
    want = jnp.where(filled_all, jnp.arange(count), count + jnp.cumsum(jnp.where(filled_all, 0, 1)))
    want = want.reshape(mp_count, own)
    want_own = jnp.where(core == 0, want[0], want[1])
    want_other = jnp.where(core == 0, want[1], want[0])
    mask = jnp.where(core == 0, filled[0], filled[1])[:, None]
    pick_own = (want_own[:, None] == place[None, :]).astype(BF)
    pick_other = (want_other[:, None] == place[None, :]).astype(BF)

    x = mm(pick_own, tokens, ((1,), (0,)))
    ct = mm(pick_own, cotangent, ((1,), (0,))).astype(BF)

    nhat_1, inv_1 = norm_stats(x)
    normed = (nhat_1 * first_gain + first_shift).astype(BF)
    normed_wide = normed.astype(F32)
    gate = jax.nn.sigmoid(jnp.sum(normed_wide * router, axis=-1, keepdims=True))

    def exchange(value):
        return lax.all_to_all(
            value.reshape(rows, half, width), ("dp", "mp"), split_axis=0, concat_axis=0, tiled=True
        ).reshape(slots, width)

    received = exchange(jnp.where(mask, normed[:slots], jnp.asarray(EMPTY, BF)))
    valid = received[:, :1].astype(F32) < 0.5 * EMPTY
    buffer = jnp.where(valid, received, jnp.zeros((), BF))
    valid_keys = valid[:, 0]

    def canonical(pair):
        return jnp.where(
            core == 0, jnp.concatenate(pair, axis=1), jnp.concatenate(pair[::-1], axis=1)
        )

    def uncanonical(value):
        first, second = jnp.split(value, 2, axis=1)
        return jnp.where(core == 0, first, second), jnp.where(core == 0, second, first)

    saved = []
    contexts = []
    for w in w_attend_2:
        proj = mm(buffer, w.reshape(width, 3 * heads_cols), ((1,), (0,))).astype(BF)
        q, k, v = (proj.reshape(slots, 3, heads, HD)[:, i] for i in range(3))
        scores = jnp.einsum("qhd,khd->hqk", q, k, preferred_element_type=F32) * HD ** (-0.5)
        scores = jnp.where(valid_keys[None, None, :], scores, MASKED_SCORE)
        peak = jnp.max(scores, axis=-1, keepdims=True)
        weights = jnp.exp(scores - peak)
        probs = (weights / jnp.sum(weights, axis=-1, keepdims=True)).astype(BF)
        context = jnp.einsum("hqk,khd->qhd", probs, v, preferred_element_type=F32)
        contexts.append(context.reshape(slots, heads_cols).astype(BF))
        saved.append((q, k, v, probs))
    gathered = exchange(canonical(contexts))
    gathered = uncanonical(jnp.where(mask, gathered, jnp.zeros((), BF)))
    attended_slots = sum(mm(g, w, ((1,), (0,))) for g, w in zip(gathered, w_output_2))
    attended = jnp.pad(attended_slots, ((0, own - slots), (0, 0)))
    mixed = x + gate * attended
    nhat_2, inv_2 = norm_stats(mixed)
    hidden_two = (nhat_2 * second_gain + second_shift).astype(BF)
    mlp_out = 0.0
    hidden_grad = 0.0
    expand_parts = []
    reduce_parts = []
    for w_e, w_r in zip(w_expand_2, w_reduce_2):
        pre = mm(hidden_two, w_e, ((1,), (0,)))
        act_grad = mm(ct, w_r, ((1,), (1,)))
        gelu, pull = jax.vjp(lambda v: jax.nn.gelu(v, approximate=False), pre)
        act = gelu.astype(BF)
        pre_grad = pull(act_grad)[0].astype(BF)
        mlp_out = mlp_out + mm(act, w_r, ((1,), (0,)))
        hidden_grad = hidden_grad + mm(pre_grad, w_e, ((1,), (1,)))
        expand_parts.append(mm(hidden_two, pre_grad, ((0,), (0,))).astype(BF))
        reduce_parts.append(mm(ct, act, ((0,), (0,))).astype(BF))
    layer_own = (mixed + mlp_out).astype(BF)

    def both(parts):
        return (parts[0].astype(F32) + swap(parts[1]).astype(F32)).astype(BF)

    expand_sum = scatter_sum(both(expand_parts), order_a)
    reduce_sum = scatter_sum(both(reduce_parts), order_b)

    second_gain_grad = jnp.sum(hidden_grad * nhat_2, axis=0)
    second_shift_grad = jnp.sum(hidden_grad, axis=0)
    mixed_grad = ct.astype(F32) + norm_pull(hidden_grad * second_gain, nhat_2, inv_2)
    attended_grad = (gate * mixed_grad)[:slots].astype(BF)
    logit_grad = jnp.sum(mixed_grad * attended, axis=-1, keepdims=True) * gate * (1.0 - gate)
    router_grad = jnp.sum(logit_grad * normed_wide, axis=0)
    context_grad = canonical([mm(attended_grad, w, ((1,), (1,))).astype(BF) for w in w_output_2])
    context_grad = exchange(jnp.where(mask, context_grad, jnp.zeros((), BF)))
    output_parts = [mm(attended_grad, g, ((0,), (0,))).astype(BF) for g in gathered]
    buffer_grad = 0.0
    attend_parts = []
    for upstream, w, (q, k, v, probs) in zip(uncanonical(context_grad), w_attend_2, saved):
        upstream = upstream.reshape(slots, heads, HD)
        probs_grad = jnp.einsum("qhd,khd->hqk", upstream, v, preferred_element_type=F32)
        probs_wide = probs.astype(F32)
        delta = jnp.sum(probs_wide * probs_grad, axis=-1, keepdims=True)
        scores_grad = (probs_wide * (probs_grad - delta)).astype(BF)
        v_grad = jnp.einsum("hqk,qhd->khd", probs, upstream, preferred_element_type=F32)
        q_grad = jnp.einsum("hqk,khd->qhd", scores_grad, k, preferred_element_type=F32) * HD ** (-0.5)
        k_grad = jnp.einsum("hqk,qhd->khd", scores_grad, q, preferred_element_type=F32) * HD ** (-0.5)
        proj_grad = jnp.stack([q_grad, k_grad, v_grad], axis=1).astype(BF).reshape(slots, 3 * heads_cols)
        w = w.reshape(width, 3 * heads_cols)
        buffer_grad = buffer_grad + mm(proj_grad, w, ((1,), (1,)))
        attend_parts.append(mm(buffer, proj_grad, ((0,), (0,))).astype(BF))
    late = both([jnp.concatenate(pair, axis=1) for pair in zip(attend_parts, output_parts)])
    split = late.shape[1] // 2
    late_sum = jnp.concatenate(
        [scatter_sum(late[:, :split], order_a), scatter_sum(late[:, split:], order_b)], axis=1
    )
    returned = exchange(buffer_grad.astype(BF))
    returned = jnp.where(mask, returned, jnp.zeros((), BF)).astype(F32)
    normed_grad = jnp.pad(returned, ((0, own - slots), (0, 0))) + logit_grad * router
    first_gain_grad = jnp.sum(normed_grad * nhat_1, axis=0)
    first_shift_grad = jnp.sum(normed_grad, axis=0)
    tokens_own = (mixed_grad + norm_pull(normed_grad * first_gain, nhat_1, inv_1)).astype(BF)

    vectors = jnp.stack(
        [first_gain_grad, first_shift_grad, router_grad, second_gain_grad, second_shift_grad]
    )
    vectors = vectors + swap(vectors)
    vectors = scatter_sum(vectors.T, order_a)

    def unpick(value):
        other = swap(value)
        return mm(pick_own, value, ((0,), (0,))) + mm(pick_other, other, ((0,), (0,)))

    layer_out = unpick(layer_own).astype(BF)
    tokens_grad = unpick(tokens_own)
    attend_cols = 3 * heads_cols
    return (
        layer_out,
        tokens_grad,
        vectors[:, 0],
        vectors[:, 1],
        vectors[:, 2],
        late_sum[:, :attend_cols].reshape(-1, 3, heads_cols),
        late_sum[:, attend_cols:].T,
        vectors[:, 3],
        vectors[:, 4],
        expand_sum,
        reduce_sum.T,
    )


def solution(mesh):
    in_specs = (
        P("dp", None),
        P("dp"),
        P("dp"),
        P("dp"),
        P(),
        P(),
        P(),
        P(None, None, "mp"),
        P("mp", None),
        P(),
        P(),
        P(None, "mp"),
        P("mp", None),
        P("dp", None),
    )
    out_specs = (
        P("dp", None),
        P("dp", None),
        P("dp"),
        P("dp"),
        P("dp"),
        P("dp", None, "mp"),
        P("mp", "dp"),
        P("dp"),
        P("dp"),
        P("dp", "mp"),
        P("mp", "dp"),
    )
    return jax.shard_map(shards, mesh=mesh, in_specs=in_specs, out_specs=out_specs, check_vma=False)
```

time: 958 us -> 372 us (0.39)
  waiting for transfers between devices: 581 us -> 123 us
  blocking collectives: 76.5 us -> 0 us
  local copies, waits for them, and re-layouts: 70.5 us -> 39.5 us
  other arithmetic: 67.2 us -> 41.9 us
  between operations: 16 us -> 2.29 us
  matrix products: 103 us -> 116 us
    reduce_scatter x4 -> x0, waiting for transfers between devices: 454 us -> none  [the longest x1 142 us: shards(): lax.psum_scatter(expand_grad, 'dp', scatter_dimension=0, tiled=True)]
    unnamed x1 -> x0, blocking collectives: 76.5 us -> none
    ppermute x0 -> x30, waiting for transfers between devices: none -> 69.7 us  [the longest x20 69.7 us: scatter_sum(): got = lax.ppermute(give, 'dp', [(i, i ^ 1 << step) for i in range(count)])]
    psum x3 -> x0, waiting for transfers between devices: 43.3 us -> none  [the longest x1 22.1 us: shards(): lax.psum(jnp.einsum('tf,df->td', pre_grad, w_expand, preferred_element_ty...]
    all_to_all x5 -> x4, waiting for transfers between devices: 83.5 us -> 53.1 us  [exchange(): lax.all_to_all(value.reshape(rows, half, width), ('dp', 'mp'), split_axis...]
    reduce_sum x15 -> x8, other arithmetic: 40 us -> 10.5 us  [the longest x1 2.83 us: shards(): first_gain_grad = jnp.sum(normed_grad * nhat_1, axis=0)]
    ppermute x0 -> x30, starting transfers between devices: none -> 24.4 us  [the longest x20 21.8 us: scatter_sum(): got = lax.ppermute(give, 'dp', [(i, i ^ 1 << step) for i in range(count)])]
    all_to_all x5 -> x4, starting transfers between devices: 34.9 us -> 19.3 us  [exchange(): lax.all_to_all(value.reshape(rows, half, width), ('dp', 'mp'), split_axis...]
  transfers between devices with their start and end apart: 12 -> 34, of which waited for: 10 -> 18; matrix products, arithmetic and copies ran while one was open for 7% -> 38% of each run, Pallas kernels for 0% -> 0%
where the time goes in v1:
time: 372 us; the launch traced here: 366 us
  waiting for transfers between devices  123 us (33%)
  matrix products  116 us (31%)
  starting transfers between devices  43.7 us (12%)
  other arithmetic  41.9 us (11%)
  local copies, waits for them, and re-layouts  39.5 us (11%)
    dot_general x30, matrix products, mm(): return lax.dot_general(a, b, (dims, ((), ())), preferred_element_type=F32)  97.1 us
    ppermute x20, waiting for transfers between devices, scatter_sum(): got = lax.ppermute(give, 'dp', [(i, i ^ 1 << step) for i in range(count)])  69.7 us
    all_to_all x4, waiting for transfers between devices, exchange(): lax.all_to_all(value.reshape(rows, half, width), ('dp', 'mp'), split_axis...  53.1 us
    ppermute x20, starting transfers between devices, scatter_sum(): got = lax.ppermute(give, 'dp', [(i, i ^ 1 << step) for i in range(count)])  21.8 us
    all_to_all x4, starting transfers between devices, exchange(): lax.all_to_all(value.reshape(rows, half, width), ('dp', 'mp'), split_axis...  19.3 us
    unnamed x120, local copies, waits for them, and re-layouts  11 us
    convert_element_type x4, local copies, waits for them, and re-layouts, shards(): contexts.append(context.reshape(slots, heads_cols).astype(BF))  9.31 us
  transfers between devices with their start and end apart: 34, of which 18 were waited for; matrix products, arithmetic and copies ran while one was open for 38% of the time, Pallas kernels for 0%

profile of v1, /device:TPU:0, one launch (start us, length us, event | category | flops | bytes accessed | tf_op | source)
XLA Modules:
  0.0 366.3 jit_solution(13914833755268163161)
XLA Ops:
  1.5 2.7 convert_reduce_fusion
  15.3 7.5 %all-to-all-start = ((bf16[32,11,768]{2,1,0:T(8,128)(2,1)}), bf16[32,11,768]{2,1,0:T(8,128)(2,1)S(1)}, u32[]{:S(2)}, u32[]{:S(2)}) async-start(bf16[32,11,768]{2,1,0:T(8,128)(2,1)} %reshape.339), calls=%async_computation | async-start | bytes 1572864 | tf_op jit(solution)/shard_map/all_to_all | solution.py:121
  22.8 2.6 copy.68
  25.9 17.5 %all-to-all-done = bf16[32,11,768]{2,1,0:T(8,128)(2,1)S(1)} async-done(((bf16[32,11,768]{2,1,0:T(8,128)(2,1)}), bf16[32,11,768]{2,1,0:T(8,128)(2,1)S(1)}, u32[]{:S(2)}, u32[]{:S(2)}) %all-to-all-start) | async-done | bytes 540704 | tf_op jit(solution)/shard_map/all_to_all | solution.py:121
  46.9 3.0 fusion.106
  56.4 2.4 convert_element_type.329
  58.8 2.6 convolution_convert_fusion.6
  62.3 2.9 fusion.105
  71.7 2.4 convert_element_type.334
  74.2 2.5 maximum_select_fusion
  76.6 4.0 %all-to-all-start.1 = ((bf16[32,11,768]{2,1,0:T(8,128)(2,1)}), bf16[32,11,768]{2,1,0:T(8,128)(2,1)}, u32[]{:S(2)}, u32[]{:S(2)}) async-start(bf16[32,11,768]{2,1,0:T(8,128)(2,1)} %maximum_select_fusion), calls=%async_computation.1 | async-start | bytes 1572864 | tf_op jit(solution)/shard_map/all_to_all | solution.py:121
  81.5 3.8 %fusion.58 = bf16[577,768]{1,0:T(8,128)(2,1)} fusion(bf16[1154,768]{1,0:T(8,128)(2,1)} %param.27, s32[1154]{0:T(1024)S(1)} %copy-done.48, s32[577]{0:T(1024)S(1)} %get-tuple-element.59), kind=kOutput, calls=%fused_computation.125 | convolution fusion | flops 1023866880 | bytes 2665740 | tf_op jit(solution)/shard_map/dot_general | solution.py:16
  85.3 15.8 %all-to-all-done.1 = bf16[32,11,768]{2,1,0:T(8,128)(2,1)} async-done(((bf16[32,11,768]{2,1,0:T(8,128)(2,1)}), bf16[32,11,768]{2,1,0:T(8,128)(2,1)}, u32[]{:S(2)}, u32[]{:S(2)}) %all-to-all-start.1) | async-done | bytes 540704 | tf_op jit(solution)/shard_map/all_to_all | solution.py:121
  112.2 9.7 %add_convert_fusion.4 = (bf16[577,1536]{1,0:T(8,128)(2,1)S(1)}, f32[577,1536]{1,0:T(8,128)S(1)}) fusion(f32[577,1536]{1,0:T(8,128)S(1)} %fusion.107, bf16[577,768]{1,0:T(8,128)(2,1)S(1)} %copy-done.28, bf16[1536,768]{1,0:T(8,128)(2,1)S(1)} %copy-done.55), kind=kOutput, calls=%fused_computation.27 | convolution fusion | flops 1425125376 | bytes 12108288 | tf_op jit(solution)/shard_map/dot_general | solution.py:16
  121.9 3.9 %fusion.109 = f32[577,1536]{1,0:T(8,128)S(1)} fusion(bf16[577,768]{1,0:T(8,128)(2,1)S(1)} %add_convert_fusion.9, bf16[768,1536]{1,0:T(8,128)(2,1)} %collective-permute-done.2), kind=kOutput, calls=%fused_computation.286 | convolution fusion | flops 1361313792 | bytes 6790656 | tf_op jit(solution)/shard_map/dot_general | solution.py:16
  128.2 11.2 %add_convert_fusion.3 = (bf16[577,1536]{1,0:T(8,128)(2,1)S(1)}, f32[577,1536]{1,0:T(8,128)S(1)}) fusion(f32[577,1536]{1,0:T(8,128)S(1)} %fusion.109, bf16[577,768]{1,0:T(8,128)(2,1)S(1)} %copy-done.28, bf16[1536,768]{1,0:T(8,128)(2,1)} %collective-permute-done.3), kind=kOutput, calls=%fused_computation.26 | convolution fusion | flops 1425125376 | bytes 12108288 | tf_op jit(solution)/shard_map/dot_general | solution.py:16
  140.2 3.5 convolution_convert_fusion.2
  143.7 4.2 %add_convert_fusion.8 = bf16[577,768]{1,0:T(8,128)(2,1)} fusion(f32[577,768]{1,0:T(8,128)S(1)} %get-tuple-element.49, f32[577,768]{1,0:T(8,128)S(1)} %fusion.108, bf16[577,1536]{1,0:T(8,128)(2,1)S(1)} %multiply_convert_fusion, bf16[1536,768]{1,0:T(8,128)(2,1)} %collective-permute-done.3), kind=kOutput, calls=%fused_computation.98 | convolution fusion | flops 1362643200 | bytes 8563200 | tf_op jit(solution)/shard_map/dot_general | solution.py:16
  149.5 3.4 convolution_convert_fusion.4
  153.0 3.8 %multiply_reduce_fusion = (f32[768]{0:T(1024)S(1)}, f32[577]{0:T(1024)S(1)}, f32[577]{0:T(1024)S(1)}, f32[768]{0:T(1024)S(1)}, f32[577,768]{1,0:T(8,128)S(1)}) fusion(f32[577,768]{1,0:T(8,128)S(1)} %get-tuple-element.49, f32[577]{0:T(1024)S(1)} %add_rsqrt_fusion, f32[577]{0:T(1024)S(1)} %broadcast_multiply_fusion.4, f32[768]{0:T(1024)S(1)} %copy-done.44, ...), kind=kOutput, calls=%fused_computation.88 | convolution fusion | flops 1365742336 | bytes 9467920 | tf_op jit(solution)/shard_map/dot_general | solution.py:16
  166.3 2.6 fusion.75
  168.8 4.0 %all-to-all-start.2 = ((bf16[32,11,768]{2,1,0:T(8,128)(2,1)}), bf16[32,11,768]{2,1,0:T(8,128)(2,1)}, u32[]{:S(2)}, u32[]{:S(2)}) async-start(bf16[32,11,768]{2,1,0:T(8,128)(2,1)} %fusion.75), calls=%async_computation.2 | async-start | bytes 1572864 | tf_op jit(solution)/shard_map/all_to_all | solution.py:121
  173.5 2.6 convolution_convert_fusion.8
  176.1 2.6 convolution_convert_fusion.9
  178.7 5.0 %fusion.6 = f32[1154,768]{1,0:T(8,128)} fusion(bf16[577,768]{1,0:T(8,128)(2,1)} %add_convert_fusion.8, s32[1154]{0:T(1024)S(1)} %copy-done.48, s32[577]{0:T(1024)S(1)} %get-tuple-element.59), kind=kOutput, calls=%fused_computation.9 | convolution fusion | flops 1023423744 | bytes 4438284 | tf_op jit(solution)/shard_map/dot_general | solution.py:16
  183.6 9.8 %all-to-all-done.2 = bf16[32,11,768]{2,1,0:T(8,128)(2,1)} async-done(((bf16[32,11,768]{2,1,0:T(8,128)(2,1)}), bf16[32,11,768]{2,1,0:T(8,128)(2,1)}, u32[]{:S(2)}, u32[]{:S(2)}) %all-to-all-start.2) | async-done | bytes 540704 | tf_op jit(solution)/shard_map/all_to_all | solution.py:121
  199.3 2.4 fusion.72
  214.6 2.4 fusion.61
  218.1 3.8 %all-to-all-start.3 = ((bf16[32,11,768]{2,1,0:T(8,128)(2,1)}), bf16[32,11,768]{2,1,0:T(8,128)(2,1)S(1)}, u32[]{:S(2)}, u32[]{:S(2)}) async-start(bf16[32,11,768]{2,1,0:T(8,128)(2,1)} %reshape.349), calls=%async_computation.3 | async-start | bytes 1572864 | tf_op jit(solution)/shard_map/all_to_all | solution.py:121
  222.0 5.5 %fusion.24 = bf16[1154,768]{1,0:T(8,128)(2,1)} fusion(f32[1154,768]{1,0:T(8,128)} %fusion.6, bf16[577,768]{1,0:T(8,128)(2,1)} %collective-permute-done.4, s32[1154]{0:T(1024)S(1)} %copy-done.48, s32[577]{0:T(1024)S(1)} %copy-done.52), kind=kOutput, calls=%fused_computation.58 | convolution fusion | flops 1025196288 | bytes 6210828 | tf_op jit(solution)/shard_map/dot_general | solution.py:16
  227.5 2.4 convolution_convert_fusion
  230.0 2.5 convolution_convert_fusion.1
  232.5 9.9 %all-to-all-done.3 = bf16[32,11,768]{2,1,0:T(8,128)(2,1)S(1)} async-done(((bf16[32,11,768]{2,1,0:T(8,128)(2,1)}), bf16[32,11,768]{2,1,0:T(8,128)(2,1)S(1)}, u32[]{:S(2)}, u32[]{:S(2)}) %all-to-all-start.3) | async-done | bytes 540704 | tf_op jit(solution)/shard_map/all_to_all | solution.py:121
  242.8 2.8 multiply_reduce_fusion.1
  245.8 2.7 pad_maximum_fusion
  250.7 2.3 collective-permute-done.7
  258.3 2.7 add_convert_fusion.7
  266.2 3.8 %add_convert_fusion.1 = bf16[768,1536]{1,0:T(8,128)(2,1)S(1)} fusion(bf16[768,1536]{1,0:T(8,128)(2,1)} %collective-permute-done.20, bf16[577,768]{1,0:T(8,128)(2,1)S(1)} %copy-done.27, bf16[577,1536]{1,0:T(8,128)(2,1)S(1)} %copy-done.58), kind=kOutput, calls=%fused_computation.14 | convolution fusion | flops 1367212032 | bytes 7377408 | tf_op jit(solution)/shard_map/dot_general | solution.py:16
  271.5 4.0 %add_convert_fusion = bf16[768,1536]{1,0:T(8,128)(2,1)S(1)} fusion(bf16[768,1536]{1,0:T(8,128)(2,1)} %collective-permute-done.25, bf16[577,768]{1,0:T(8,128)(2,1)S(1)} %copy-done.29, bf16[577,1536]{1,0:T(8,128)(2,1)S(1)} %copy-done.20), kind=kOutput, calls=%fused_computation.13 | convolution fusion | flops 1367212032 | bytes 7377408 | tf_op jit(solution)/shard_map/dot_general | solution.py:16
  276.8 3.8 %convolution_add_fusion = f32[1154,768]{1,0:T(8,128)} fusion(f32[1154,768]{1,0:T(8,128)S(1)} %fusion.2, bf16[577,768]{1,0:T(8,128)(2,1)S(1)} %collective-permute-done.5, s32[1154]{0:T(1024)S(1)} %copy-done.49, s32[577]{0:T(1024)S(1)} %copy-done.52), kind=kOutput, calls=%fused_computation.16 | convolution fusion | flops 1024310016 | bytes 7983372 | tf_op jit(solution)/shard_map/dot_general | solution.py:16
  280.6 2.3 add_convert_fusion.2
  285.1 14.1 %collective-permute-done.21 = bf16[2,2,2,1,48,1536]{5,4,3,2,1,0:T(8,128)(2,1)S(1)} collective-permute-done((bf16[2,2,2,1,48,1536]{5,4,3,2,1,0:T(8,128)(2,1)S(1)}, bf16[2,2,2,1,48,1536]{5,4,3,2,1,0:T(8,128)(2,1)S(1)}, u32[]{:S(2)}, u32[]{:S(2)}) %collective-permute-start.21) | collective-permute-done | bytes 1179680 | tf_op jit(solution)/shard_map/ppermute | solution.py:46
  300.6 4.0 %collective-permute-done.26 = bf16[2,2,1,2,48,1536]{5,4,3,2,1,0:T(8,128)(2,1)S(1)} collective-permute-done((bf16[2,2,1,2,48,1536]{5,4,3,2,1,0:T(8,128)(2,1)S(1)}, bf16[2,2,1,2,48,1536]{5,4,3,2,1,0:T(8,128)(2,1)S(1)}, u32[]{:S(2)}, u32[]{:S(2)}) %collective-permute-start.26) | collective-permute-done | bytes 1179680 | tf_op jit(solution)/shard_map/ppermute | solution.py:46
  306.0 11.2 %collective-permute-done.16 = bf16[2,2,1,2,48,768]{5,4,3,2,1,0:T(8,128)(2,1)S(1)} collective-permute-done((bf16[2,2,1,2,48,768]{5,4,3,2,1,0:T(8,128)(2,1)S(1)}, bf16[2,2,1,2,48,768]{5,4,3,2,1,0:T(8,128)(2,1)S(1)}, u32[]{:S(2)}, u32[]{:S(2)}) %collective-permute-start.16) | collective-permute-done | bytes 589856 | tf_op jit(solution)/shard_map/ppermute | solution.py:46
  320.1 9.7 %collective-permute-done.22 = bf16[2,2,1,1,48,1536]{5,4,3,2,1,0:T(8,128)(2,1)S(1)} collective-permute-done((bf16[2,2,1,1,48,1536]{5,4,3,2,1,0:T(8,128)(2,1)S(1)}, bf16[2,2,1,1,48,1536]{5,4,3,2,1,0:T(8,128)(2,1)S(1)}, u32[]{:S(2)}, u32[]{:S(2)}) %collective-permute-start.22) | collective-permute-done | bytes 589856 | tf_op jit(solution)/shard_map/ppermute | solution.py:46
  335.3 6.4 %collective-permute-done.23 = bf16[2,1,1,1,48,1536]{5,4,3,2,1,0:T(8,128)(2,1)S(1)} collective-permute-done((bf16[2,1,1,1,48,1536]{5,4,3,2,1,0:T(8,128)(2,1)S(1)}, bf16[2,1,1,1,48,1536]{5,4,3,2,1,0:T(8,128)(2,1)S(1)}, u32[]{:S(2)}, u32[]{:S(2)}) %collective-permute-start.23) | collective-permute-done | bytes 294944 | tf_op jit(solution)/shard_map/ppermute | solution.py:46
  341.8 7.8 %collective-permute-done.28 = bf16[2,1,1,1,48,1536]{5,4,3,2,1,0:T(8,128)(2,1)S(1)} collective-permute-done((bf16[2,1,1,1,48,1536]{5,4,3,2,1,0:T(8,128)(2,1)S(1)}, bf16[2,1,1,1,48,1536]{5,4,3,2,1,0:T(8,128)(2,1)S(1)}, u32[]{:S(2)}, u32[]{:S(2)}) %collective-permute-start.28) | collective-permute-done | bytes 294944 | tf_op jit(solution)/shard_map/ppermute | solution.py:46
  355.0 7.3 %collective-permute-done.19 = bf16[1,1,1,1,48,768]{5,4,3,2,1,0:T(8,128)(2,1)S(1)} collective-permute-done((bf16[1,1,1,1,48,768]{5,4,3,2,1,0:T(8,128)(2,1)S(1)}, bf16[1,1,1,1,48,768]{5,4,3,2,1,0:T(8,128)(2,1)S(1)}, u32[]{:S(2)}, u32[]{:S(2)}) %collective-permute-start.19) | collective-permute-done | bytes 73760 | tf_op jit(solution)/shard_map/ppermute | solution.py:46
  (324 shorter events, 114.4 us)
Async XLA Ops:
  8.7 169.9 %copy-start.53 = (s32[577]{0:T(1024)}, s32[577]{0:T(1024)S(1)}, u32[]{:S(2)}) copy-start(s32[577]{0:T(1024)S(1)} %get-tuple-element.59) | copy-start | bytes 6928
  12.0 91.3 %copy-start.45 = (pred[352]{0:T(512)(128)(4,1)}, pred[352]{0:T(512)(128)(4,1)S(1)}, u32[]{:S(2)}) copy-start(pred[352]{0:T(512)(128)(4,1)S(1)} %select_n.187) | copy-start | bytes 1060
  15.3 28.1 %all-to-all-start = ((bf16[32,11,768]{2,1,0:T(8,128)(2,1)}), bf16[32,11,768]{2,1,0:T(8,128)(2,1)S(1)}, u32[]{:S(2)}, u32[]{:S(2)}) async-start(bf16[32,11,768]{2,1,0:T(8,128)(2,1)} %reshape.339), calls=%async_computation | async-start | bytes 1572864 | tf_op jit(solution)/shard_map/all_to_all | solution.py:121
  25.5 20.6 %copy-start.7 = (bf16[768,3,384]{0,2,1:T(8,128)(2,1)}, bf16[768,3,384]{0,2,1:T(8,128)(2,1)S(1)}, u32[]{:S(2)}) copy-start(bf16[768,3,384]{0,2,1:T(8,128)(2,1)S(1)} %copy.68) | copy-start | bytes 5308420
  25.5 33.4 %collective-permute-start = (bf16[768,3,384]{0,2,1:T(8,128)(2,1)S(1)}, bf16[768,3,384]{0,2,1:T(8,128)(2,1)}, u32[]{:S(2)}, u32[]{:S(2)}) collective-permute-start(bf16[768,3,384]{0,2,1:T(8,128)(2,1)S(1)} %copy.68), channel_id=1, source_target_pairs={{0,1},{1,0},{2,3},{3,2},{4,5},{5,4},{6,7},{7,6},{8,9},{9,8},{10,11... | collective-permute-start | bytes 5308424 | tf_op jit(solution)/shard_map/ppermute | solution.py:30
  71.7 9.8 %copy-start.48 = (s32[1154]{0:T(1024)S(1)}, s32[1154]{0:T(1024)}, u32[]{:S(2)}) copy-start(s32[1154]{0:T(1024)} %copy-done.47) | copy-start | bytes 13852
  76.6 24.6 %all-to-all-start.1 = ((bf16[32,11,768]{2,1,0:T(8,128)(2,1)}), bf16[32,11,768]{2,1,0:T(8,128)(2,1)}, u32[]{:S(2)}, u32[]{:S(2)}) async-start(bf16[32,11,768]{2,1,0:T(8,128)(2,1)} %maximum_select_fusion), calls=%async_computation.1 | async-start | bytes 1572864 | tf_op jit(solution)/shard_map/all_to_all | solution.py:121
  80.6 25.7 %collective-permute-start.1 = (bf16[384,768]{1,0:T(8,128)(2,1)}, bf16[384,768]{1,0:T(8,128)(2,1)}, u32[]{:S(2)}, u32[]{:S(2)}) collective-permute-start(bf16[384,768]{1,0:T(8,128)(2,1)} %param.22), channel_id=1, source_target_pairs={{0,1},{1,0},{2,3},{3,2},{4,5},{5,4},{6,7},{7,6},{8,9},{9,8},{10,11... | collective-permute-start | bytes 1769480 | tf_op jit(solution)/shard_map/ppermute | solution.py:30
  81.0 40.9 %collective-permute-start.2 = (bf16[768,1536]{1,0:T(8,128)(2,1)}, bf16[768,1536]{1,0:T(8,128)(2,1)}, u32[]{:S(2)}, u32[]{:S(2)}) collective-permute-start(bf16[768,1536]{1,0:T(8,128)(2,1)} %param.25), channel_id=1, source_target_pairs={{0,1},{1,0},{2,3},{3,2},{4,5},{5,4},{6,7},{7,6},{8,9},{9,8},{10,11... | collective-permute-start | bytes 7077896 | tf_op jit(solution)/shard_map/ppermute | solution.py:30
  81.2 47.0 %collective-permute-start.3 = (bf16[1536,768]{1,0:T(8,128)(2,1)}, bf16[1536,768]{1,0:T(8,128)(2,1)}, u32[]{:S(2)}, u32[]{:S(2)}) collective-permute-start(bf16[1536,768]{1,0:T(8,128)(2,1)} %param.26), channel_id=1, source_target_pairs={{0,1},{1,0},{2,3},{3,2},{4,5},{5,4},{6,7},{7,6},{8,9},{9,8},{10,11... | collective-permute-start | bytes 7077896 | tf_op jit(solution)/shard_map/ppermute | solution.py:30
  85.3 22.4 %copy-start.43 = (f32[577]{0:T(1024)}, f32[577]{0:T(1024)S(1)}, u32[]{:S(2)}) copy-start(f32[577]{0:T(1024)S(1)} %add_divide_fusion) | copy-start | bytes 6928
  109.9 39.6 %copy-start.26 = (bf16[577,768]{1,0:T(8,128)(2,1)}, bf16[577,768]{1,0:T(8,128)(2,1)S(1)}, u32[]{:S(2)}) copy-start(bf16[577,768]{1,0:T(8,128)(2,1)S(1)} %add_convert_fusion.9) | copy-start | bytes 2658820
  121.9 26.0 %copy-start.57 = (bf16[577,1536]{1,0:T(8,128)(2,1)}, bf16[577,1536]{1,0:T(8,128)(2,1)S(1)}, u32[]{:S(2)}) copy-start(bf16[577,1536]{1,0:T(8,128)(2,1)S(1)} %get-tuple-element.46) | copy-start | bytes 5317636
  147.9 74.1 %collective-permute-start.4 = (bf16[577,768]{1,0:T(8,128)(2,1)}, bf16[577,768]{1,0:T(8,128)(2,1)}, u32[]{:S(2)}, u32[]{:S(2)}) collective-permute-start(bf16[577,768]{1,0:T(8,128)(2,1)} %add_convert_fusion.8), channel_id=1, source_target_pairs={{0,1},{1,0},{2,3},{3,2},{4,5},{5,4},{6,7},{7,6},{8,9},{9,8},{10,11... | collective-permute-start | bytes 2658824 | tf_op jit(solution)/shard_map/ppermute | solution.py:30
  168.8 24.6 %all-to-all-start.2 = ((bf16[32,11,768]{2,1,0:T(8,128)(2,1)}), bf16[32,11,768]{2,1,0:T(8,128)(2,1)}, u32[]{:S(2)}, u32[]{:S(2)}) async-start(bf16[32,11,768]{2,1,0:T(8,128)(2,1)} %fusion.75), calls=%async_computation.2 | async-start | bytes 1572864 | tf_op jit(solution)/shard_map/all_to_all | solution.py:121
  172.9 93.3 %collective-permute-start.20 = (bf16[768,1536]{1,0:T(8,128)(2,1)}, bf16[768,1536]{1,0:T(8,128)(2,1)}, u32[]{:S(2)}, u32[]{:S(2)}) collective-permute-start(bf16[768,1536]{1,0:T(8,128)(2,1)} %convolution_convert_fusion.4), channel_id=1, source_target_pairs={{0,1},{1,0},{2,3},{3,2},{4,5},{5,4},{6,7},{7,6},{8,9},{9,8},{10,11... | collective-permute-start | bytes 7077896 | tf_op jit(solution)/shard_map/ppermute | solution.py:30
  173.3 97.8 %collective-permute-start.25 = (bf16[768,1536]{1,0:T(8,128)(2,1)}, bf16[768,1536]{1,0:T(8,128)(2,1)}, u32[]{:S(2)}, u32[]{:S(2)}) collective-permute-start(bf16[768,1536]{1,0:T(8,128)(2,1)} %convolution_convert_fusion.2), channel_id=1, source_target_pairs={{0,1},{1,0},{2,3},{3,2},{4,5},{5,4},{6,7},{7,6},{8,9},{9,8},{10,11... | collective-permute-start | bytes 7077896 | tf_op jit(solution)/shard_map/ppermute | solution.py:30
  218.1 24.3 %all-to-all-start.3 = ((bf16[32,11,768]{2,1,0:T(8,128)(2,1)}), bf16[32,11,768]{2,1,0:T(8,128)(2,1)S(1)}, u32[]{:S(2)}, u32[]{:S(2)}) async-start(bf16[32,11,768]{2,1,0:T(8,128)(2,1)} %reshape.349), calls=%async_computation.3 | async-start | bytes 1572864 | tf_op jit(solution)/shard_map/all_to_all | solution.py:121
  229.9 12.7 %copy-start.46 = (pred[352]{0:T(512)(128)(4,1)S(1)}, pred[352]{0:T(512)(128)(4,1)}, u32[]{:S(2)}) copy-start(pred[352]{0:T(512)(128)(4,1)} %copy-done.45) | copy-start | bytes 1060
  229.9 12.8 %copy-start.10 = (bf16[577,768]{1,0:T(8,128)(2,1)S(1)}, bf16[577,768]{1,0:T(8,128)(2,1)}, u32[]{:S(2)}) copy-start(bf16[577,768]{1,0:T(8,128)(2,1)} %copy-done.9) | copy-start | bytes 2658820
  229.9 12.8 %copy-start.34 = (f32[577]{0:T(1024)S(1)}, f32[577]{0:T(1024)}, u32[]{:S(2)}) copy-start(f32[577]{0:T(1024)} %copy-done.33) | copy-start | bytes 6928
  229.9 12.8 %copy-start.38 = (f32[577]{0:T(1024)S(1)}, f32[577]{0:T(1024)}, u32[]{:S(2)}) copy-start(f32[577]{0:T(1024)} %copy-done.37) | copy-start | bytes 6928
  229.9 12.8 %copy-start.40 = (f32[768]{0:T(1024)S(1)}, f32[768]{0:T(1024)}, u32[]{:S(2)}) copy-start(f32[768]{0:T(1024)} %param.20) | copy-start | bytes 9220
  230.0 12.8 %copy-start.42 = (f32[768]{0:T(1024)S(1)}, f32[768]{0:T(1024)}, u32[]{:S(2)}) copy-start(f32[768]{0:T(1024)} %param.18) | copy-start | bytes 9220
  245.7 3.3 collective-permute-start.6
  248.5 32.1 %collective-permute-start.11 = (bf16[768,1536]{1,0:T(8,128)(2,1)}, bf16[768,1536]{1,0:T(8,128)(2,1)}, u32[]{:S(2)}, u32[]{:S(2)}) collective-permute-start(bf16[768,1536]{1,0:T(8,128)(2,1)} %pad_maximum_fusion), channel_id=1, source_target_pairs={{0,1},{1,0},{2,3},{3,2},{4,5},{5,4},{6,7},{7,6},{8,9},{9,8},{10,11... | collective-permute-start | bytes 7077896 | tf_op jit(solution)/shard_map/ppermute | solution.py:30
  249.1 3.8 %collective-permute-start.7 = (f32[2,2,2,1,48,5]{4,3,2,1,0,5:T(1,128)S(1)}, f32[2,2,2,1,48,5]{4,3,2,1,0,5:T(1,128)S(1)}, u32[]{:S(2)}, u32[]{:S(2)}) collective-permute-start(f32[2,2,2,1,48,5]{4,3,2,1,0,5:T(1,128)S(1)} %constant_dynamic-slice_fusion.21), channel_id=1, source_target_pairs={{0,2},{2,0},{4,6},{6,4},{8,10},{10,8},{12,14},{14,12},{16,18},{18,... | collective-permute-start | bytes 23048 | tf_op jit(solution)/shard_map/ppermute | solution.py:46
  253.0 3.7 %collective-permute-start.8 = (f32[2,2,1,1,48,5]{4,3,2,1,0,5:T(1,128)S(1)}, f32[2,2,1,1,48,5]{4,3,2,1,0,5:T(1,128)S(1)}, u32[]{:S(2)}, u32[]{:S(2)}) collective-permute-start(f32[2,2,1,1,48,5]{4,3,2,1,0,5:T(1,128)S(1)} %constant_dynamic-slice_fusion.20), channel_id=1, source_target_pairs={{0,4},{2,6},{4,0},{6,2},{8,12},{10,14},{12,8},{14,10},{16,20},{18,... | collective-permute-start | bytes 11528 | tf_op jit(solution)/shard_map/ppermute | solution.py:46
  256.8 4.2 %collective-permute-start.9 = (f32[2,1,1,1,48,5]{4,3,2,1,0,5:T(1,128)S(1)}, f32[2,1,1,1,48,5]{4,3,2,1,0,5:T(1,128)S(1)}, u32[]{:S(2)}, u32[]{:S(2)}) collective-permute-start(f32[2,1,1,1,48,5]{4,3,2,1,0,5:T(1,128)S(1)} %constant_dynamic-slice_fusion.18), channel_id=1, source_target_pairs={{0,8},{2,10},{4,12},{6,14},{8,0},{10,2},{12,4},{14,6},{16,24},{18,... | collective-permute-start | bytes 5768 | tf_op jit(solution)/shard_map/ppermute | solution.py:46
  261.1 4.6 %collective-permute-start.10 = (f32[1,1,1,1,48,5]{4,3,2,1,0,5:T(1,128)S(1)}, f32[1,1,1,1,48,5]{4,3,2,1,0,5:T(1,128)S(1)}, u32[]{:S(2)}, u32[]{:S(2)}) collective-permute-start(f32[1,1,1,1,48,5]{4,3,2,1,0,5:T(1,128)S(1)} %constant_dynamic-slice_fusion.16), channel_id=1, source_target_pairs={{0,16},{2,18},{4,20},{6,22},{8,24},{10,26},{12,28},{14,30},{16,0},... | collective-permute-start | bytes 2888 | tf_op jit(solution)/shard_map/ppermute | solution.py:46
  263.9 12.9 %collective-permute-start.5 = (bf16[577,768]{1,0:T(8,128)(2,1)S(1)}, bf16[577,768]{1,0:T(8,128)(2,1)S(1)}, u32[]{:S(2)}, u32[]{:S(2)}) collective-permute-start(bf16[577,768]{1,0:T(8,128)(2,1)S(1)} %add_convert_fusion.7), channel_id=1, source_target_pairs={{0,1},{1,0},{2,3},{3,2},{4,5},{5,4},{6,7},{7,6},{8,9},{9,8},{10,11... | collective-permute-start | bytes 2658824 | tf_op jit(solution)/shard_map/ppermute | solution.py:30
  270.1 29.0 %collective-permute-start.21 = (bf16[2,2,2,1,48,1536]{5,4,3,2,1,0:T(8,128)(2,1)S(1)}, bf16[2,2,2,1,48,1536]{5,4,3,2,1,0:T(8,128)(2,1)S(1)}, u32[]{:S(2)}, u32[]{:S(2)}) collective-permute-start(bf16[2,2,2,1,48,1536]{5,4,3,2,1,0:T(8,128)(2,1)S(1)} %constant_dynamic-slice_fusion.7), channel_id=1, source_target_pairs={{0,2},{2,0},{4,6},{6,4},{8,10},{10,8},{12,14},{14,12},{16,18},{18,... | collective-permute-start | bytes 3538952 | tf_op jit(solution)/shard_map/ppermute | solution.py:46
  275.6 29.0 %collective-permute-start.26 = (bf16[2,2,1,2,48,1536]{5,4,3,2,1,0:T(8,128)(2,1)S(1)}, bf16[2,2,1,2,48,1536]{5,4,3,2,1,0:T(8,128)(2,1)S(1)}, u32[]{:S(2)}, u32[]{:S(2)}) collective-permute-start(bf16[2,2,1,2,48,1536]{5,4,3,2,1,0:T(8,128)(2,1)S(1)} %constant_dynamic-slice_fusion.3), channel_id=1, source_target_pairs={{0,4},{2,6},{4,0},{6,2},{8,12},{10,14},{12,8},{14,10},{16,20},{18,... | collective-permute-start | bytes 3538952 | tf_op jit(solution)/shard_map/ppermute | solution.py:46
  283.1 34.1 %collective-permute-start.16 = (bf16[2,2,1,2,48,768]{5,4,3,2,1,0:T(8,128)(2,1)S(1)}, bf16[2,2,1,2,48,768]{5,4,3,2,1,0:T(8,128)(2,1)S(1)}, u32[]{:S(2)}, u32[]{:S(2)}) collective-permute-start(bf16[2,2,1,2,48,768]{5,4,3,2,1,0:T(8,128)(2,1)S(1)} %constant_dynamic-slice_fusion.11), channel_id=1, source_target_pairs={{0,4},{2,6},{4,0},{6,2},{8,12},{10,14},{12,8},{14,10},{16,20},{18,... | collective-permute-start | bytes 1769480 | tf_op jit(solution)/shard_map/ppermute | solution.py:46
  284.1 34.3 %collective-permute-start.12 = (bf16[2,2,2,1,48,768]{5,4,3,2,1,0:T(8,128)(2,1)S(1)}, bf16[2,2,2,1,48,768]{5,4,3,2,1,0:T(8,128)(2,1)S(1)}, u32[]{:S(2)}, u32[]{:S(2)}) collective-permute-start(bf16[2,2,2,1,48,768]{5,4,3,2,1,0:T(8,128)(2,1)S(1)} %constant_dynamic-slice_fusion.15), channel_id=1, source_target_pairs={{0,2},{2,0},{4,6},{6,4},{8,10},{10,8},{12,14},{14,12},{16,18},{18,... | collective-permute-start | bytes 1769480 | tf_op jit(solution)/shard_map/ppermute | solution.py:46
  299.5 30.3 %collective-permute-start.22 = (bf16[2,2,1,1,48,1536]{5,4,3,2,1,0:T(8,128)(2,1)S(1)}, bf16[2,2,1,1,48,1536]{5,4,3,2,1,0:T(8,128)(2,1)S(1)}, u32[]{:S(2)}, u32[]{:S(2)}) collective-permute-start(bf16[2,2,1,1,48,1536]{5,4,3,2,1,0:T(8,128)(2,1)S(1)} %constant_dynamic-slice_fusion.6), channel_id=1, source_target_pairs={{0,4},{2,6},{4,0},{6,2},{8,12},{10,14},{12,8},{14,10},{16,20},{18,... | collective-permute-start | bytes 1769480 | tf_op jit(solution)/shard_map/ppermute | solution.py:46
  305.0 26.0 %collective-permute-start.27 = (bf16[2,2,1,1,48,1536]{5,4,3,2,1,0:T(8,128)(2,1)S(1)}, bf16[2,2,1,1,48,1536]{5,4,3,2,1,0:T(8,128)(2,1)S(1)}, u32[]{:S(2)}, u32[]{:S(2)}) collective-permute-start(bf16[2,2,1,1,48,1536]{5,4,3,2,1,0:T(8,128)(2,1)S(1)} %constant_dynamic-slice_fusion.2), channel_id=1, source_target_pairs={{0,2},{2,0},{4,6},{6,4},{8,10},{10,8},{12,14},{14,12},{16,18},{18,... | collective-permute-start | bytes 1769480 | tf_op jit(solution)/shard_map/ppermute | solution.py:46
  317.4 15.0 %collective-permute-start.17 = (bf16[2,2,1,1,48,768]{5,4,3,2,1,0:T(8,128)(2,1)S(1)}, bf16[2,2,1,1,48,768]{5,4,3,2,1,0:T(8,128)(2,1)S(1)}, u32[]{:S(2)}, u32[]{:S(2)}) collective-permute-start(bf16[2,2,1,1,48,768]{5,4,3,2,1,0:T(8,128)(2,1)S(1)} %constant_dynamic-slice_fusion.10), channel_id=1, source_target_pairs={{0,2},{2,0},{4,6},{6,4},{8,10},{10,8},{12,14},{14,12},{16,18},{18,... | collective-permute-start | bytes 884744 | tf_op jit(solution)/shard_map/ppermute | solution.py:46
  318.6 15.3 %collective-permute-start.13 = (bf16[2,2,1,1,48,768]{5,4,3,2,1,0:T(8,128)(2,1)S(1)}, bf16[2,2,1,1,48,768]{5,4,3,2,1,0:T(8,128)(2,1)S(1)}, u32[]{:S(2)}, u32[]{:S(2)}) collective-permute-start(bf16[2,2,1,1,48,768]{5,4,3,2,1,0:T(8,128)(2,1)S(1)} %constant_dynamic-slice_fusion.14), channel_id=1, source_target_pairs={{0,4},{2,6},{4,0},{6,2},{8,12},{10,14},{12,8},{14,10},{16,20},{18,... | collective-permute-start | bytes 884744 | tf_op jit(solution)/shard_map/ppermute | solution.py:46
  330.0 11.6 %collective-permute-start.23 = (bf16[2,1,1,1,48,1536]{5,4,3,2,1,0:T(8,128)(2,1)S(1)}, bf16[2,1,1,1,48,1536]{5,4,3,2,1,0:T(8,128)(2,1)S(1)}, u32[]{:S(2)}, u32[]{:S(2)}) collective-permute-start(bf16[2,1,1,1,48,1536]{5,4,3,2,1,0:T(8,128)(2,1)S(1)} %constant_dynamic-slice_fusion.5), channel_id=1, source_target_pairs={{0,8},{2,10},{4,12},{6,14},{8,0},{10,2},{12,4},{14,6},{16,24},{18,... | collective-permute-start | bytes 884744 | tf_op jit(solution)/shard_map/ppermute | solution.py:46
  331.1 18.5 %collective-permute-start.28 = (bf16[2,1,1,1,48,1536]{5,4,3,2,1,0:T(8,128)(2,1)S(1)}, bf16[2,1,1,1,48,1536]{5,4,3,2,1,0:T(8,128)(2,1)S(1)}, u32[]{:S(2)}, u32[]{:S(2)}) collective-permute-start(bf16[2,1,1,1,48,1536]{5,4,3,2,1,0:T(8,128)(2,1)S(1)} %constant_dynamic-slice_fusion.1), channel_id=1, source_target_pairs={{0,8},{2,10},{4,12},{6,14},{8,0},{10,2},{12,4},{14,6},{16,24},{18,... | collective-permute-start | bytes 884744 | tf_op jit(solution)/shard_map/ppermute | solution.py:46
  332.5 18.8 %collective-permute-start.18 = (bf16[2,1,1,1,48,768]{5,4,3,2,1,0:T(8,128)(2,1)S(1)}, bf16[2,1,1,1,48,768]{5,4,3,2,1,0:T(8,128)(2,1)S(1)}, u32[]{:S(2)}, u32[]{:S(2)}) collective-permute-start(bf16[2,1,1,1,48,768]{5,4,3,2,1,0:T(8,128)(2,1)S(1)} %constant_dynamic-slice_fusion.9), channel_id=1, source_target_pairs={{0,8},{2,10},{4,12},{6,14},{8,0},{10,2},{12,4},{14,6},{16,24},{18,... | collective-permute-start | bytes 442376 | tf_op jit(solution)/shard_map/ppermute | solution.py:46
  334.0 19.5 %collective-permute-start.14 = (bf16[2,1,1,1,48,768]{5,4,3,2,1,0:T(8,128)(2,1)S(1)}, bf16[2,1,1,1,48,768]{5,4,3,2,1,0:T(8,128)(2,1)S(1)}, u32[]{:S(2)}, u32[]{:S(2)}) collective-permute-start(bf16[2,1,1,1,48,768]{5,4,3,2,1,0:T(8,128)(2,1)S(1)} %constant_dynamic-slice_fusion.13), channel_id=1, source_target_pairs={{0,8},{2,10},{4,12},{6,14},{8,0},{10,2},{12,4},{14,6},{16,24},{18,... | collective-permute-start | bytes 442376 | tf_op jit(solution)/shard_map/ppermute | solution.py:46
  341.7 22.8 %collective-permute-start.24 = (bf16[1,1,1,1,48,1536]{5,4,3,2,1,0:T(8,128)(2,1)S(1)}, bf16[1,1,1,1,48,1536]{5,4,3,2,1,0:T(8,128)(2,1)S(1)}, u32[]{:S(2)}, u32[]{:S(2)}) collective-permute-start(bf16[1,1,1,1,48,1536]{5,4,3,2,1,0:T(8,128)(2,1)S(1)} %constant_dynamic-slice_fusion.4), channel_id=1, source_target_pairs={{0,16},{2,18},{4,20},{6,22},{8,24},{10,26},{12,28},{14,30},{16,0},... | collective-permute-start | bytes 442376 | tf_op jit(solution)/shard_map/ppermute | solution.py:46
  349.6 16.4 %copy-start.1 = (bf16[1154,768]{1,0:T(8,128)(2,1)S(1)}, bf16[1154,768]{1,0:T(8,128)(2,1)}, u32[]{:S(2)}) copy-start(bf16[1154,768]{1,0:T(8,128)(2,1)} %param.14) | copy-start | bytes 5317636
  349.7 15.5 %collective-permute-start.29 = (bf16[1,1,1,1,48,1536]{5,4,3,2,1,0:T(8,128)(2,1)S(1)}, bf16[1,1,1,1,48,1536]{5,4,3,2,1,0:T(8,128)(2,1)S(1)}, u32[]{:S(2)}, u32[]{:S(2)}) collective-permute-start(bf16[1,1,1,1,48,1536]{5,4,3,2,1,0:T(8,128)(2,1)S(1)} %constant_dynamic-slice_fusion), channel_id=1, source_target_pairs={{0,16},{2,18},{4,20},{6,22},{8,24},{10,26},{12,28},{14,30},{16,0},... | collective-permute-start | bytes 442376 | tf_op jit(solution)/shard_map/ppermute | solution.py:46
  351.3 11.0 %collective-permute-start.19 = (bf16[1,1,1,1,48,768]{5,4,3,2,1,0:T(8,128)(2,1)S(1)}, bf16[1,1,1,1,48,768]{5,4,3,2,1,0:T(8,128)(2,1)S(1)}, u32[]{:S(2)}, u32[]{:S(2)}) collective-permute-start(bf16[1,1,1,1,48,768]{5,4,3,2,1,0:T(8,128)(2,1)S(1)} %constant_dynamic-slice_fusion.8), channel_id=1, source_target_pairs={{0,16},{2,18},{4,20},{6,22},{8,24},{10,26},{12,28},{14,30},{16,0},... | collective-permute-start | bytes 221192 | tf_op jit(solution)/shard_map/ppermute | solution.py:46
  353.6 9.5 %collective-permute-start.15 = (bf16[1,1,1,1,48,768]{5,4,3,2,1,0:T(8,128)(2,1)S(1)}, bf16[1,1,1,1,48,768]{5,4,3,2,1,0:T(8,128)(2,1)S(1)}, u32[]{:S(2)}, u32[]{:S(2)}) collective-permute-start(bf16[1,1,1,1,48,768]{5,4,3,2,1,0:T(8,128)(2,1)S(1)} %constant_dynamic-slice_fusion.12), channel_id=1, source_target_pairs={{0,16},{2,18},{4,20},{6,22},{8,24},{10,26},{12,28},{14,30},{16,0},... | collective-permute-start | bytes 221192 | tf_op jit(solution)/shard_map/ppermute | solution.py:46
  (46 other events, 136.5 us)
